TPU v7x, 256 devices: a whole 4x4x8 slice. The times are simulated.
256 devices in a mesh: front: 8 (over y, x_lo), row: 4 (over x_hi, core), col: 8 (over z).
Axes of the slice: x: 4 (x_hi: 2, x_lo: 2; x = x_hi * 2 + x_lo), y: 4, z: 8, core: 2. Of those that a mesh axis runs over, the one named last changes fastest.
Arguments:
- front_slab: float32 [8, 32, 4, 128, 1, 8, 256], P('front', None, 'row', None, None, 'col'), as said below
- child_keep: float32 [8, 8, 4, 128, 1, 8, 256], P('front', None, 'row', None, None, 'col'), may hold values from -1 to 1
- child_give: float32 [8, 8, 4, 128, 1, 8, 256], P('front', None, 'row', None, None, 'col'), may hold values from -1 to 1
- map_keep: int32 [8, 8, 4], replicated, may hold values from 0 to 127, as said below
- map_give: int32 [8, 8, 4], replicated, may hold values from 0 to 127, as said below
Outputs:
- factored: float32 [8, 32, 4, 128, 1, 8, 256], P('front', None, 'row', None, None, 'col')
Inputs may be any that keep to these rules, and one draw needn't show every extreme that they name: `map_keep`: row blocks of one child map to distinct parent row blocks. Parent row block p is held by row index p mod 4. Of the child row blocks held by one row index, at most 4 map to blocks held by any one row index, and every row index sends exactly 4 of them to one row index. `map_give`: as for map_keep, for the child held by each front's devices. `front_slab`: the leading 256 x 256 block of every front, after the children are added, is symmetric-part diagonally dominant with a positive diagonal.
All inputs are finite; a program needn't handle non-finite values.
Results may differ from a plain program's by a relative error of at most 0.0001.
Values sent between devices are 32-bit elements; how exact they have to be, the bound alone decides.
A program may use at most 128 MiB of HBM per device.

v0:
```python
import jax
import jax.numpy as jnp
from jax import lax
from jax.sharding import PartitionSpec as P

precise = lax.Precision.HIGHEST


def from_partner(array, axis, bit):
    return lax.ppermute(array, axis, [(i, i ^ 1 << bit) for i in range(lax.axis_size(axis))])


def from_root(value, axis, source):
    kept = jnp.where(lax.axis_index(axis) == source, value, 0).astype(value.dtype)
    return lax.psum(kept, axis)


def routing(table, groups):
    target = table % groups
    position = table // groups
    markers = (target[:, :, None] == jnp.arange(groups, dtype=jnp.int32)[None, None, :]).astype(
        jnp.int32
    )
    before = jnp.cumsum(markers, axis=0) - markers
    seat_index = jnp.sum(before * markers, axis=2)
    return (target, seat_index, position)


def pack_blocks(child, table, row_id, groups, capacity):
    target, seat_index, position = routing(table, groups)
    target_mine = lax.dynamic_index_in_dim(target, row_id, 1, keepdims=False)
    slot_mine = lax.dynamic_index_in_dim(seat_index, row_id, 1, keepdims=False)
    select = (target_mine[None, None, :] == jnp.arange(groups)[:, None, None]) & (
        slot_mine[None, None, :] == jnp.arange(capacity)[None, :, None]
    )
    return jnp.einsum("dsj,jix->dsix", select.astype(jnp.float32), child, precision=precise)


def unpack_blocks(received, table, row_id, groups, capacity, blocks):
    target, seat_index, position = routing(table, groups)
    arrival = (target == row_id)[None, :, :, None]
    where_to = position[None, :, :, None] == jnp.arange(blocks)[:, None, None, None]
    slot_match = seat_index[None, :, :, None] == jnp.arange(capacity)[None, None, None, :]
    scatter = jnp.sum((arrival & where_to & slot_match).astype(jnp.float32), axis=1)
    return jnp.einsum("bsk,skix->bix", scatter, received, precision=precise)


def local(front_slab, child_keep, child_give, map_keep, map_give):
    groups = lax.axis_size("row")
    columns = lax.axis_size("col")
    row_id = lax.axis_index("row")
    col_id = lax.axis_index("col")
    front_id = lax.axis_index("front")
    blocks = front_slab.shape[1]
    block_rows = front_slab.shape[3]
    layers = front_slab.shape[4]
    panel_width = front_slab.shape[6]
    slab_width = layers * panel_width
    pieces = child_keep.shape[1]
    capacity = pieces // 2
    front_local = front_slab.reshape(blocks, block_rows, slab_width)
    kept_child = child_keep.reshape(pieces, block_rows, slab_width)
    kept_table = lax.dynamic_index_in_dim(map_keep, front_id, 0, keepdims=False)
    moved_table = lax.dynamic_index_in_dim(
        map_give, jnp.bitwise_xor(front_id, 1), 0, keepdims=False
    )
    kept_send = pack_blocks(kept_child, kept_table, row_id, groups, capacity)
    moved_child = from_partner(child_give, "front", 0).reshape(pieces, block_rows, slab_width)
    moved_send = pack_blocks(moved_child, moved_table, row_id, groups, capacity)
    kept_recv = lax.all_to_all(kept_send, "row", split_axis=0, concat_axis=0, tiled=True)
    moved_recv = lax.all_to_all(moved_send, "row", split_axis=0, concat_axis=0, tiled=True)
    assembled = front_local + unpack_blocks(kept_recv, kept_table, row_id, groups, capacity, blocks)
    assembled = assembled + unpack_blocks(moved_recv, moved_table, row_id, groups, capacity, blocks)
    panel_rows = from_root(assembled, "col", 0)
    halves = panel_width // block_rows
    col_blocks = jnp.arange(layers) * columns + col_id
    top_blocks = layers * columns * halves // groups
    leading_rows = panel_rows[:top_blocks][:, None]
    window = lax.all_gather(leading_rows, "row", axis=1, tiled=True).reshape(
        -1, panel_width, panel_width
    )
    diagonal = window[0]
    needed = jnp.take(window, col_blocks, axis=0)
    lower_factor = jnp.linalg.cholesky(diagonal)

    def factor_rows(matrix, row_index):
        solved = lax.linalg.triangular_solve(
            lower_factor, matrix, left_side=False, lower=True, transpose_a=True
        )
        leading = jnp.take(lower_factor, jnp.minimum(row_index, panel_width - 1), axis=0)
        return jnp.where(row_index[:, None] < panel_width, leading, solved)

    mine_index = (
        (jnp.arange(blocks)[:, None] * groups + row_id) * block_rows
        + jnp.arange(block_rows)[None, :]
    ).reshape(-1)
    factor_mine = factor_rows(panel_rows.reshape(-1, panel_width), mine_index)
    need_index = (col_blocks[:, None] * panel_width + jnp.arange(panel_width)[None, :]).reshape(-1)
    factor_need = factor_rows(needed.reshape(-1, panel_width), need_index)
    update = jnp.dot(factor_mine, factor_need.T, precision=precise)
    result = assembled.reshape(-1, slab_width) - update
    result = jnp.where(mine_index[:, None] < panel_width, jnp.float32(0.0), result)
    result = result.reshape(-1, layers, panel_width)
    panel_part = jnp.where(col_id == 0, factor_mine, result[:, 0])
    result = jnp.concatenate([panel_part[:, None], result[:, 1:]], axis=1)
    return result.reshape(front_slab.shape)


def solution(mesh):
    placed = (
        P("front", None, "row", None, None, "col", None),
        P("front", None, "row", None, None, "col", None),
        P("front", None, "row", None, None, "col", None),
        P(),
        P(),
    )
    return jax.shard_map(
        local,
        mesh=mesh,
        in_specs=placed,
        out_specs=P("front", None, "row", None, None, "col", None),
        check_vma=False,
    )
```

profile of v0, /device:TPU:1, one launch (start us, length us, event | category | flops | bytes accessed | tf_op | source)
XLA Modules:
  0.0 377.1 jit_solution(15274043264344354012)
XLA Ops:
  6.5 0.8 broadcast_compare_fusion
  7.4 0.7 reduce_window_sum.19
  8.2 4.4 %fusion.13 = f32[4,4,128,256]{3,1,2,0:T(4,128)} fusion(f32[1,8,1,128,1,1,256]{6,5,4,3,2,1,0:T(1,128)} %param.6, pred[4,4,8,1]{2,0,1,3:T(4,128)(4,1)S(1)} %and_bitcast_fusion.1), kind=kOutput, calls=%fused_computation.25 | convolution fusion | flops 50331648 | bytes 3145856 | tf_op jit(solution)/shard_map/dsj,jix->dsix/dot_general | solution.py:36
  12.6 6.8 %all-to-all-start = ((f32[4,4,128,256]{3,1,2,0:T(4,128)}), f32[4,4,128,256]{3,1,2,0:T(4,128)S(1)}, u32[]{:S(2)}, u32[]{:S(2)}) async-start(f32[4,4,128,256]{3,1,2,0:T(4,128)} %fusion.13), calls=%async_computation | async-start | bytes 4194304 | tf_op jit(solution)/shard_map/all_to_all | solution.py:70
  19.4 1.6 copy.70
  21.0 0.7 reduce_window_sum.20
  21.8 43.2 %collective-permute-done = f32[1,8,1,128,1,1,256]{6,1,3,5,4,2,0:T(8,128)S(1)} collective-permute-done((f32[1,8,1,128,1,1,256]{6,1,3,5,4,2,0:T(8,128)}, f32[1,8,1,128,1,1,256]{6,1,3,5,4,2,0:T(8,128)S(1)}, u32[]{:S(2)}, u32[]{:S(2)}) %collective-permute-start) | collective-permute-done | bytes 1048608 | tf_op jit(solution)/shard_map/ppermute | solution.py:10
  65.1 2.7 fusion.11
  67.8 1.3 copy-done.1
  69.1 5.6 %all-to-all-start.1 = ((f32[4,4,128,256]{3,1,2,0:T(4,128)}), f32[4,4,128,256]{3,1,2,0:T(4,128)S(1)}, u32[]{:S(2)}, u32[]{:S(2)}) async-start(f32[4,4,128,256]{3,1,2,0:T(4,128)} %fusion.11), calls=%async_computation.1 | async-start | bytes 4194304 | tf_op jit(solution)/shard_map/all_to_all | solution.py:71
  74.8 0.7 add_select_fusion
  75.9 6.4 %fusion.40 = f32[32,128,256,1]{2,0,1,3:T(8,128)} fusion(f32[4,4,128,256]{3,1,2,0:T(4,128)} %copy-done.1, f32[32,4,4]{0,2,1:T(4,128)S(1)} %convert_reduce_fusion.1), kind=kOutput, calls=%fused_computation.72 | convolution fusion | flops 201326592 | bytes 6293504 | tf_op jit(solution)/shard_map/bsk,skix->bix/dot_general | solution.py:45
  82.3 18.8 %all-to-all-done.1 = f32[4,4,128,256]{3,1,2,0:T(4,128)S(1)} async-done(((f32[4,4,128,256]{3,1,2,0:T(4,128)}), f32[4,4,128,256]{3,1,2,0:T(4,128)S(1)}, u32[]{:S(2)}, u32[]{:S(2)}) %all-to-all-start.1) | async-done | bytes 2097184 | tf_op jit(solution)/shard_map/all_to_all | solution.py:71
  101.1 9.8 %broadcast_select_fusion = (f32[32,128,256]{2,0,1:T(8,128)}, f32[32,128,256]{2,0,1:T(8,128)}) fusion(pred[]{:T(512)S(6)} %eq.219, f32[4,4,128,256]{3,1,2,0:T(4,128)S(1)} %all-to-all-done.1, f32[32,4,4]{0,2,1:T(4,128)S(1)} %convert_reduce_fusion, f32[32,128,256,1]{2,0,1,3:T(8,128)} %fusion.40, f32[1,32,1,128,1,1,256]{6,5,4,3,2,1,0:T(1,128)} %param.5), kind=kOutput, calls=%fused_computation.18 | convolution fusion | flops 204472320 | bytes 18876416 | tf_op jit(solution)/shard_map/bsk,skix->bix/dot_general | solution.py:45
  110.9 0.2 all-gather.3.cloned.1.call-start
  111.2 109.6 %all-reduce.3.cloned.1.call-done = f32[32,128,256]{2,0,1:T(8,128)} async-done(((f32[32,128,256]{2,0,1:T(8,128)}), f32[32,128,256]{2,0,1:T(8,128)}) %all-reduce.3.cloned.1.call-update) | async-done | bytes 4194320 | tf_op jit(solution)/shard_map/psum | solution.py:15
  220.8 2.1 slice.84
  223.3 6.6 %copy.79 = f32[32,128,256]{2,1,0:T(8,128)} copy(f32[32,128,256]{2,0,1:T(8,128)} %get-tuple-element.47) | data formatting | bytes 8388608 | tf_op jit(solution)/shard_map/add | solution.py:73
  229.9 5.7 %copy.82 = f32[4096,256]{0,1:T(8,128)} copy(f32[4096,256]{1,0:T(8,128)} %bitcast.160) | data formatting | bytes 8388608 | tf_op jit(solution)/shard_map/reshape | solution.py:101
  235.6 6.6 %copy.78 = f32[32,128,256]{2,1,0:T(8,128)} copy(f32[32,128,256]{2,0,1:T(8,128)} %all-reduce.3.cloned.1.call-done) | data formatting | bytes 8388608 | tf_op jit(solution)/shard_map/psum | solution.py:15
  242.2 9.1 %all-gather.3.cloned.1.call-done = f32[4,512,256]{2,0,1:T(4,128)} async-done(((f32[4,128,256]{2,0,1:T(4,128)}), f32[4,512,256]{2,0,1:T(4,128)}) %all-gather.3.cloned.1.call-update) | async-done | bytes 2097168 | tf_op jit(solution)/shard_map/all_gather | solution.py:79
  251.4 2.0 copy.74
  253.4 0.1 copy.102
  253.6 11.7 %cholesky.51 = f32[128,128]{1,0:T(8,128)S(1)} custom-call(f32[128,128]{1,0:T(8,128)S(1)} %cholesky.121), custom_call_target="Cholesky" | custom-call | tf_op jit(solution)/shard_map/jit(cholesky)/cholesky | solution.py:84
  265.3 0.6 compare_reduce_fusion.1
  266.0 9.8 %custom-call.16 = f32[1,128,128]{1,2,0:T(8,128)S(1)} custom-call(f32[1,128,128]{2,1,0:T(8,128)S(1)} %get-tuple-element.45), custom_call_target="InvertDiagBlocksLowerTriangular" | custom-call | tf_op jit(solution)/shard_map/jit(cholesky)/cholesky | solution.py:84
  275.8 0.2 constant_dynamic-update-slice_fusion
  276.0 0.3 convolution_subtract_fusion.3
  276.3 11.9 %cholesky.107 = f32[128,128]{1,0:T(8,128)S(1)} custom-call(f32[128,128]{1,0:T(8,128)S(1)} %convolution_subtract_fusion.3), custom_call_target="Cholesky" | custom-call | tf_op jit(solution)/shard_map/jit(cholesky)/cholesky | solution.py:84
  288.3 0.7 compare_reduce_fusion
  290.3 3.9 %while.2 = (s32[]{:T(128)}, f32[256,256]{1,0:T(8,128)S(1)}, s32[2,2]{1,0:T(2,128)S(1)}, f32[2,128,128]{2,1,0:T(8,128)S(1)}, s32[]{:T(128)}) while((s32[]{:T(128)}, f32[256,256]{1,0:T(8,128)S(1)}, s32[2,2]{1,0:T(2,128)S(1)}, f32[2,128,128]{2,1,0:T(8,128)S(1)}, s32[]{:T(128)}) %tuple.36), condition=%wide.while_cond, body=%wide.while_body.sunk | while | flops 2 | bytes 131189 | solution.py:87
  290.3 0.6 fusion.67
  290.9 1.3 bitcast_dynamic-update-slice_fusion.2
  292.2 0.6 fusion.67
  292.8 1.3 bitcast_dynamic-update-slice_fusion.2
  294.2 19.7 %custom-call.17 = f32[2,128,128]{1,2,0:T(8,128)S(1)} custom-call(f32[2,128,128]{2,1,0:T(8,128)S(1)} %get-tuple-element.12), custom_call_target="InvertDiagBlocksLowerTriangular" | custom-call | tf_op jit(solution)/shard_map/triangular_solve | solution.py:87
  313.8 0.3 fusion.22
  314.2 0.4 convolution_subtract_fusion.2
  314.7 0.3 fusion.30
  314.9 3.7 fusion.6
  318.7 3.5 convolution_subtract_fusion.1
  322.2 3.4 fusion.31
  325.7 1.0 gather_fusion.1
  326.6 16.1 %gather_fusion = f32[4096,256]{1,0:T(8,128)} fusion(f32[256,256]{1,0:T(8,128)S(1)} %get-tuple-element.33, s32[4096]{0:T(1024)S(1)} %broadcast_clamp_fusion), kind=kCustom, calls=%fused_computation | custom fusion | bytes 8404992 | tf_op jit(solution)/shard_map/jit(_take)/gather | solution.py:90
  342.8 5.9 %copy.77 = f32[4096,256]{0,1:T(8,128)} copy(f32[4096,256]{1,0:T(8,128)} %gather_fusion) | data formatting | bytes 8388608 | tf_op jit(solution)/shard_map/jit(_take)/gather | solution.py:90
  348.7 11.3 %fusion.5 = f32[32,8,32,128]{3,1,2,0:T(8,128)S(1)} fusion(f32[4096,256]{0,1:T(8,128)} %copy.82, f32[4096,128]{0,1:T(8,128)} %fusion.31, f32[4096,128]{0,1:T(8,128)S(1)} %fusion.6, f32[4096,256]{0,1:T(8,128)} %copy.77, pred[4096]{0:T(1024)(128)(4,1)S(1)} %compare_and_fusion, pred[4096]{0:T(1024)(128)(4,1)S(1)} %fusion.36, pred[]{:T(512)S(6)} %eq.219, ...), kind=kOutput, calls=%fused_computation.14 | convolution fusion | flops 3230859264 | bytes 17310208 | tf_op jit(solution)/shard_map/dot_general | solution.py:100
  359.9 2.7 copy.104
  362.6 7.2 %copy.84 = f32[1,32,1,128,1,1,256]{6,5,4,3,2,1,0:T(1,128)} copy(f32[1,32,1,128,1,1,256]{3,1,6,5,4,2,0:T(8,128)} %bitcast.161) | data formatting | bytes 8388608 | tf_op jit(solution)/shard_map/reshape;broadcast_in_dim | solution.py:106
  (52 shorter events, 1.2 us)
Async XLA Ops:
  6.5 12.9 %copy-start.2 = (f32[1,8,1,128,1,1,256]{6,5,4,3,2,1,0:T(1,128)S(1)}, f32[1,8,1,128,1,1,256]{6,5,4,3,2,1,0:T(1,128)}, u32[]{:S(2)}) copy-start(f32[1,8,1,128,1,1,256]{6,5,4,3,2,1,0:T(1,128)} %param.7) | copy-start | bytes 3145732
  12.6 55.2 %all-to-all-start = ((f32[4,4,128,256]{3,1,2,0:T(4,128)}), f32[4,4,128,256]{3,1,2,0:T(4,128)S(1)}, u32[]{:S(2)}, u32[]{:S(2)}) async-start(f32[4,4,128,256]{3,1,2,0:T(4,128)} %fusion.13), calls=%async_computation | async-start | bytes 4194304 | tf_op jit(solution)/shard_map/all_to_all | solution.py:70
  21.0 44.1 %collective-permute-start = (f32[1,8,1,128,1,1,256]{6,1,3,5,4,2,0:T(8,128)}, f32[1,8,1,128,1,1,256]{6,1,3,5,4,2,0:T(8,128)S(1)}, u32[]{:S(2)}, u32[]{:S(2)}) collective-permute-start(f32[1,8,1,128,1,1,256]{6,1,3,5,4,2,0:T(8,128)} %copy.70), channel_id=1, source_target_pairs={{0,32},{32,0},{64,96},{96,64},{128,160},{160,128},{192,224},{224,1... | collective-permute-start | bytes 3145736 | tf_op jit(solution)/shard_map/ppermute | solution.py:10
  67.8 1.3 copy-start.1
  69.1 32.0 %all-to-all-start.1 = ((f32[4,4,128,256]{3,1,2,0:T(4,128)}), f32[4,4,128,256]{3,1,2,0:T(4,128)S(1)}, u32[]{:S(2)}, u32[]{:S(2)}) async-start(f32[4,4,128,256]{3,1,2,0:T(4,128)} %fusion.11), calls=%async_computation.1 | async-start | bytes 4194304 | tf_op jit(solution)/shard_map/all_to_all | solution.py:71
  74.8 146.0 %all-reduce.3.cloned.1.call-start = ((), (), s32[]{:S(2)}) async-start(), calls=%async_computation.2 | async-start | bytes 8388608 | tf_op jit(solution)/shard_map/psum | solution.py:15
  110.9 140.4 %all-gather.3.cloned.1.call-start = ((), (), s32[]{:S(2)}) async-start(), calls=%async_computation.3 | async-start | bytes 2621440 | tf_op jit(solution)/shard_map/all_gather | solution.py:79
  314.7 4.0 %copy-start = (f32[32,128,256]{2,1,0:T(8,128)S(1)}, f32[32,128,256]{2,1,0:T(8,128)}, u32[]{:S(2)}) copy-start(f32[32,128,256]{2,1,0:T(8,128)} %copy.78) | copy-start | bytes 12582916
Sparse Core Ops, SparseCore 0:
  111.1 109.6 all-reduce.2
  223.1 28.2 all-gather.2
where the time goes:
time: 385 us; the launch traced here: 377 us
  waiting for transfers between devices  181 us (47%)
  local copies, waits for them, and re-layouts  63 us (16%)
  other arithmetic  58.3 us (15%)
  matrix products  46.8 us (12%)
  between operations  15.4 us (4%)
  starting transfers between devices  12.7 us (3%)
    psum x1, waiting for transfers between devices, from_root(): return lax.psum(kept, axis)  110 us
    ppermute x1, waiting for transfers between devices, from_partner(): lax.ppermute(array, axis, [(i, i ^ 1 << bit) for i in range(lax.axis_size...  43.2 us
    another operation x7, other arithmetic, local(): lower_factor = jnp.linalg.cholesky(diagonal)  34.8 us
    gather x3, local copies, waits for them, and re-layouts, factor_rows(): jnp.take(lower_factor, jnp.minimum(row_index, panel_width - 1), axis=0)  23 us
    another operation x3, other arithmetic, factor_rows(): lax.linalg.triangular_solve(lower_factor, matrix, left_side=False, lower=...  19.7 us
    all_to_all x1, waiting for transfers between devices, local(): lax.all_to_all(moved_send, 'row', split_axis=0, concat_axis=0, tiled=True)  18.8 us
    dot_general x2, matrix products, unpack_blocks(): return jnp.einsum('bsk,skix->bix', scatter, received, precision=precise)  16.3 us
    another operation x6, matrix products, factor_rows(): lax.linalg.triangular_solve(lower_factor, matrix, left_side=False, lower=...  11.7 us
  transfers between devices with their start and end apart: 5, of which 4 were waited for; matrix products, arithmetic and copies ran while one was open for 8% of the time, Pallas kernels for 0%

commit v1 on v0

v1 whole, which is shorter than its diff:
```python
import functools

import jax
import jax.numpy as jnp
from jax import lax
from jax.experimental import pallas as pl
from jax.experimental.pallas import tpu as pltpu
from jax.sharding import PartitionSpec as P

F32 = jnp.float32
BF16 = jnp.bfloat16
precise = lax.Precision.HIGHEST

CHUNKS = (8, 8, 16, 16, 16, 16, 16, 16, 16)
STARTS = tuple(sum(CHUNKS[:i]) for i in range(len(CHUNKS)))
NCH = len(CHUNKS)
WINDOW = 3
PARTS = 32
SKEW = 2


def place():
    front = lax.axis_index("front")
    row = lax.axis_index("row")
    col = lax.axis_index("col")
    x = (row // 2) * 2 + front % 2
    return x, front // 2, col, row % 2


def device(x, y, z, core):
    x = lax.rem(x + 4, 4)
    z = lax.rem(z + 8, 8)
    return {"front": y * 2 + x % 2, "row": (x // 2) * 2 + core, "col": z}


def row_of(x, core):
    return (lax.rem(x + 4, 4) // 2) * 2 + core


def exchange_kernel(
    inv,
    front_hbm,
    keep_hbm,
    give_hbm,
    panel_out,
    slab_out,
    window_out,
    slab,
    panel,
    win,
    load_sem,
    own_sem,
    xs,
    xr,
    ms,
    mr,
    zs,
    zr,
    ws,
    wr,
    out_sem,
    *pools,
):
    x, y, z, core = place()
    row = row_of(x, core)
    mate = device(x, y, z, 1 - core)
    far = device(x + 2, y, z, core)
    far_mate = device(x + 2, y, z, 1 - core)
    up = device(x + 1, y, z, core)
    down = device(x - 1, y, z, core)
    nxt = device(x, y, z + 1, core)
    prv = device(x, y, z - 1, core)
    row_far = lax.rem(row + 2, 4)
    row_mate = row_of(x, 1 - core)
    row_mate_far = lax.rem(row_mate + 2, 4)
    row_up = row_of(x + 1, core)
    row_down = row_of(x - 1, core)
    row_up_mate = row_of(x + 1, 1 - core)
    row_down_mate = row_of(x - 1, 1 - core)

    load = pltpu.make_async_copy(front_hbm, slab, load_sem)
    load.start()

    barrier = pltpu.get_barrier_semaphore()
    for target in (mate, far, far_mate, up, down, nxt, prv):
        pl.semaphore_signal(barrier, 1, device_id=target)
    pl.semaphore_wait(barrier, 7)

    def rows(j):
        return pl.ds(2 * STARTS[j], 2 * CHUNKS[j])

    def eight(base):
        return pl.ds(base, 8)

    def remote(src, dst, s, r, dev):
        return pltpu.make_async_remote_copy(src, dst, s, r, device_id=dev)

    def send_x(j):
        pool = pools[j]
        keep = keep_hbm.at[:, rows(j)]
        give = give_hbm.at[:, rows(j)]
        mine = pool.at[eight(8 * row)]
        given = pool.at[eight(32 + 8 * row)]
        return (
            remote(keep, mine, xs.at[0, j], xr.at[0, j], far),
            remote(give, given, xs.at[1, j], xr.at[1, j], up),
            remote(give, given, xs.at[2, j], xr.at[2, j], down),
        )

    def recv_x(j):
        pool = pools[j]
        give = give_hbm.at[:, rows(j)]
        return (
            remote(give, pool.at[eight(8 * row_far)], xs.at[0, j], xr.at[0, j], far),
            remote(give, pool.at[eight(32 + 8 * row_down)], xs.at[1, j], xr.at[1, j], down),
            remote(give, pool.at[eight(32 + 8 * row_up)], xs.at[2, j], xr.at[2, j], up),
        )

    def own_copy(j):
        return pltpu.make_async_copy(
            keep_hbm.at[:, rows(j)], pools[j].at[eight(8 * row)], own_sem.at[j]
        )

    def own_relay(j):
        mine = pools[j].at[eight(8 * row)]
        return remote(keep_hbm.at[:, rows(j)], mine, ms.at[0, j], mr.at[0, j], mate)

    def relays(j):
        out = []
        for p, base in ((1, 8 * row_far), (2, 32 + 8 * row_down), (3, 32 + 8 * row_up)):
            part = pools[j].at[eight(base)]
            out.append(remote(part, part, ms.at[p, j], mr.at[p, j], mate))
        return out

    def relayed(j):
        out = []
        for p, base in (
            (0, 8 * row_mate),
            (1, 8 * row_mate_far),
            (2, 32 + 8 * row_down_mate),
            (3, 32 + 8 * row_up_mate),
        ):
            part = pools[j].at[eight(base)]
            out.append(remote(part, part, ms.at[p, j], mr.at[p, j], mate))
        return out

    def begin_x(j):
        for c in send_x(j):
            c.start()
        own_copy(j).start()
        own_relay(j).start()

    def arrive_x(j):
        for c in recv_x(j):
            c.wait_recv()
        for c in relays(j):
            c.start()

    def assemble(j):
        own_copy(j).wait()
        for c in relayed(j):
            c.wait_recv()
        pool = pools[j]

        def one(b, carry):
            kept = pool[inv[b]]
            moved = pool[inv[32 + b]]
            slab[b, rows(j), :] = slab[b, rows(j), :] + kept + moved
            return carry

        lax.fori_loop(0, 32, one, 0, unroll=4)

    def part(ref, way, t):
        j8 = t // 2
        g = t % 2
        return ref.at[pl.ds(16 * way + 8 * g, 8), pl.ds(pl.multiple_of(16 * j8, 16), 16)]

    def hop(ref, way, t):
        return remote(
            part(ref, way, t),
            part(panel, way, t),
            zs.at[way, t],
            zr.at[way, t],
            prv if way else nxt,
        )

    for j in range(NCH):
        pools[j][64] = jnp.zeros(pools[j].shape[1:], F32)
    for j in range(WINDOW):
        begin_x(j)
    load.wait()

    @pl.when(z == 0)
    def _():
        for j in range(NCH):
            arrive_x(j)
            if j + WINDOW < NCH:
                begin_x(j + WINDOW)
            assemble(j)

            def launch(t, carry):
                for way in (0, 1):
                    hop(slab, way, t).start()
                return carry

            lax.fori_loop(STARTS[j] // 4, (STARTS[j] + CHUNKS[j]) // 4, launch, 0)

    @pl.when(z != 0)
    def _():
        total = PARTS + SKEW * 6

        def step(s, carry):
            for way in (0, 1):
                lag = (7 - z) if way else (z - 1)
                t = s - SKEW * lag

                @pl.when((t >= 0) & (t < PARTS))
                def _():
                    copy = hop(panel, way, t)
                    copy.wait_recv()

                    @pl.when(lag < 6)
                    def _():
                        copy.start()

            return carry

        done = 0
        for j in range(NCH):
            until = 4 + 4 * j
            lax.fori_loop(done, until, step, 0)
            done = until
            arrive_x(j)
            if j + WINDOW < NCH:
                begin_x(j + WINDOW)
            if j:
                assemble(j - 1)
        lax.fori_loop(done, total, step, 0)
        assemble(NCH - 1)

    half = z // 2
    owner = 2 * lax.rem(z, 2)

    def spread(ref, block, slot):
        src = ref.at[block]
        out = []
        for i, dev in enumerate((mate, far, far_mate)):
            out.append(remote(src, win.at[slot], ws.at[slot // 2, i], wr.at[slot], dev))
        return out

    def share(ref):
        @pl.when(row < 2)
        def _():
            win[row] = ref[0]
            for slot in (0, 1):

                @pl.when(row == slot)
                def _():
                    for c in spread(ref, 0, slot):
                        c.start()

        for h in (0, 1):

            @pl.when(row == owner + h)
            def _():
                win[2 + h] = ref[half]
                for c in spread(ref, half, 2 + h):
                    c.start()

    @pl.when(z == 0)
    def _():
        share(slab)
        pltpu.make_async_copy(slab, panel_out, out_sem.at[0]).start()

    @pl.when(z != 0)
    def _():
        share(panel)
        pltpu.make_async_copy(panel, panel_out, out_sem.at[0]).start()

    pltpu.make_async_copy(slab, slab_out, out_sem.at[1]).start()

    for slot in range(4):
        holder = slot if slot < 2 else owner + slot - 2

        @pl.when(row != holder)
        def _():
            remote(win.at[slot], win.at[slot], ws.at[0, 0], wr.at[slot], mate).wait_recv()

    pltpu.make_async_copy(win, window_out, out_sem.at[2]).start()

    for slot in range(4):
        holder = slot if slot < 2 else owner + slot - 2

        @pl.when(row == holder)
        def _():
            for c in spread(panel, 0, slot):
                c.wait_send()

    for j in range(NCH):
        for c in send_x(j):
            c.wait_send()
        own_relay(j).wait_send()
        for c in relays(j):
            c.wait_send()

    def drain(t, carry):
        for way in (0, 1):
            last = 1 if way else 7

            @pl.when(z != last)
            def _():
                hop(panel, way, t).wait_send()

        return carry

    lax.fori_loop(0, PARTS, drain, 0)
    pltpu.make_async_copy(panel, panel_out, out_sem.at[0]).wait()
    pltpu.make_async_copy(slab, slab_out, out_sem.at[1]).wait()
    pltpu.make_async_copy(win, window_out, out_sem.at[2]).wait()


def exchange(inv, front, keep, give):
    big = jax.ShapeDtypeStruct(front.shape, F32)
    anywhere = pl.BlockSpec(memory_space=pl.ANY)
    dma = pltpu.SemaphoreType.DMA
    return pl.pallas_call(
        exchange_kernel,
        out_shape=[big, big, jax.ShapeDtypeStruct((4, 256, 128), F32)],
        in_specs=[pl.BlockSpec(memory_space=pltpu.SMEM)] + [anywhere] * 3,
        out_specs=[anywhere] * 3,
        scratch_shapes=[
            pltpu.VMEM(front.shape, F32),
            pltpu.VMEM(front.shape, F32),
            pltpu.VMEM((4, 256, 128), F32),
            dma,
            dma((NCH,)),
            dma((3, NCH)),
            dma((3, NCH)),
            dma((4, NCH)),
            dma((4, NCH)),
            dma((2, PARTS)),
            dma((2, PARTS)),
            dma((2, 3)),
            dma((4,)),
            dma((3,)),
        ]
        + [pltpu.VMEM((65, 2 * n, 128), F32) for n in CHUNKS],
        compiler_params=pltpu.CompilerParams(
            collective_id=0, has_side_effects=True, vmem_limit_bytes=56 << 20
        ),
        name="exchange",
    )(inv, front, keep, give)


def three(a):
    hi = a.astype(BF16)
    rest = a - hi.astype(F32)
    mid = rest.astype(BF16)
    low = (rest - mid.astype(F32)).astype(BF16)
    return hi, mid, low


def factor_panel(work, upper, j0, n=16):
    r = work[j0 : j0 + n, :]
    sub = lax.broadcasted_iota(jnp.int32, (n, 128), 0)
    sub2 = lax.broadcasted_iota(jnp.int32, (n, 256), 0)
    lane2 = lax.broadcasted_iota(jnp.int32, (n, 256), 1)
    g = [jnp.broadcast_to(r[:, j0 + i : j0 + i + 1], (n, 128)) for i in range(n)]
    for i in range(n):
        inv = lax.rsqrt(g[i][i : i + 1, :])
        l = g[i] * inv
        below = jnp.where(sub > i, l, 0.0)
        for m in range(i + 1, n):
            g[m] = g[m] - below * l[m : m + 1, :]
        line = r[i : i + 1, :] * jnp.concatenate([inv, inv], axis=1)
        r = jnp.where(sub2 == i, line, r - jnp.concatenate([below, below], axis=1) * line)
    r = jnp.where(lane2 >= sub2 + j0, r, 0.0)
    upper[j0 : j0 + n, :] = r
    if j0 + n < 256:
        h, m, l = three(r)
        a = jnp.concatenate([h, h, m, h, l, m], axis=0)
        b = jnp.concatenate([h, m, h, l, h, m], axis=0)
        t = lax.dot_general(a, b, (((0,), (0,)), ((), ())), preferred_element_type=F32)
        work[j0 + n :, :] = work[j0 + n :, :] - t[j0 + n :, :]


def invert_upper(u):
    i = lax.broadcasted_iota(jnp.int32, (256, 256), 0)
    j = lax.broadcasted_iota(jnp.int32, (256, 256), 1)
    inv = jnp.where(i == j, 1.0 / jnp.where(i == j, u, 1.0), 0.0)
    s = 1
    while s < 256:
        off = jnp.where((i // (2 * s) == j // (2 * s)) & (i // s < j // s), u, 0.0)
        step = jnp.dot(inv, off, precision=precise, preferred_element_type=F32)
        inv = inv - jnp.dot(step, inv, precision=precise, preferred_element_type=F32)
        s *= 2
    return inv


def square(ref, a, b):
    even, odd = pl.ds(0, 128, 2), pl.ds(1, 128, 2)
    top = jnp.concatenate([ref[a, even, :], ref[a, odd, :]], axis=1)
    low = jnp.concatenate([ref[b, even, :], ref[b, odd, :]], axis=1)
    return jnp.concatenate([top, low], axis=0)


def factor_kernel(ids, win, weight, top, work, upper):
    lead = square(win, 0, 1)
    work[...] = 0.5 * (lead + lead.T)
    for p in range(16):
        factor_panel(work, upper, 16 * p)
    u = upper[...]
    inv = invert_upper(u)

    @pl.when(ids[0] == 0)
    def _():
        weight[...] = -inv
        low = u.T
        top[...] = jnp.where(ids[1] == 0, low[:128], low[128:])

    @pl.when(ids[0] != 0)
    def _():
        mine = square(win, 2, 3)
        y = lax.dot_general(
            inv, mine, (((0,), (1,)), ((), ())), precision=precise, preferred_element_type=F32
        )
        weight[...] = jnp.dot(inv, y, precision=precise, preferred_element_type=F32)
        top[...] = jnp.zeros_like(top)


def factor(ids, win):
    vmem = pl.BlockSpec(memory_space=pltpu.VMEM)
    return pl.pallas_call(
        factor_kernel,
        out_shape=[jax.ShapeDtypeStruct((256, 256), F32), jax.ShapeDtypeStruct((128, 256), F32)],
        in_specs=[pl.BlockSpec(memory_space=pltpu.SMEM), vmem],
        out_specs=[vmem, vmem],
        scratch_shapes=[pltpu.VMEM((256, 256), F32)] * 2,
        compiler_params=pltpu.CompilerParams(vmem_limit_bytes=40 << 20),
        name="factor",
    )(ids, win)


def update_kernel(ids, panel, slab, weight, top, out):
    even, odd = pl.ds(0, 512, 2), pl.ds(1, 512, 2)
    keep = (ids[0] != 0).astype(F32)
    a = jnp.concatenate([panel[even, :], panel[odd, :]], axis=1)
    d = jnp.dot(a, weight[...], precision=precise, preferred_element_type=F32)
    out[even, :] = keep * slab[even, :] - d[:, :128]
    out[odd, :] = keep * slab[odd, :] - d[:, 128:]

    @pl.when((pl.program_id(0) == 0) & (ids[1] < 2))
    def _():
        out[pl.ds(0, 128, 2), :] = top[:, :128]
        out[pl.ds(1, 128, 2), :] = top[:, 128:]


def update(ids, panel, slab, weight, top):
    tile = pl.BlockSpec((1024, 128), lambda i: (i, 0))
    whole = pl.BlockSpec((256, 256), lambda i: (0, 0))
    return pl.pallas_call(
        update_kernel,
        grid=(8,),
        out_shape=jax.ShapeDtypeStruct((8192, 128), F32),
        in_specs=[
            pl.BlockSpec(memory_space=pltpu.SMEM),
            tile,
            tile,
            whole,
            pl.BlockSpec((128, 256), lambda i: (0, 0)),
        ],
        out_specs=tile,
        compiler_params=pltpu.CompilerParams(vmem_limit_bytes=40 << 20),
        name="update",
    )(ids, panel, slab, weight, top)


def local(front_slab, child_keep, child_give, map_keep, map_give):
    front_id = lax.axis_index("front")
    row_id = lax.axis_index("row")
    col_id = lax.axis_index("col")
    front = front_slab.reshape(32, 256, 128)
    keep = child_keep.reshape(8, 256, 128)
    give = child_give.reshape(8, 256, 128)
    kept = lax.dynamic_index_in_dim(map_keep, front_id, 0, keepdims=False)
    moved = lax.dynamic_index_in_dim(map_give, front_id ^ 1, 0, keepdims=False)
    tables = jnp.stack([kept.T.reshape(32), moved.T.reshape(32)])
    parent = jnp.arange(32, dtype=jnp.int32) * 4 + row_id
    slot = jnp.arange(64, dtype=jnp.int32).reshape(2, 1, 32)
    hit = tables[:, None, :] == parent[None, :, None]
    inv = (64 + jnp.sum(jnp.where(hit, slot - 64, 0), axis=2)).reshape(64).astype(jnp.int32)
    ids = jnp.stack([col_id, row_id]).astype(jnp.int32)
    panel, slab, win = exchange(inv, front, keep, give)
    weight, top = factor(ids, win)
    out = update(ids, panel.reshape(8192, 128), slab.reshape(8192, 128), weight, top)
    return out.reshape(front_slab.shape)


def solution(mesh):
    spec = P("front", None, "row", None, None, "col", None)
    return jax.shard_map(
        local,
        mesh=mesh,
        in_specs=(spec, spec, spec, P(), P()),
        out_specs=spec,
        check_vma=False,
    )
```

time: 385 us -> 135 us (0.35)
  the two profiles are of different devices: /device:TPU:1 before, /device:TPU:33 now
where the time goes in v1:
time: 135 us
  Pallas kernels  127 us (94%)
  local copies, waits for them, and re-layouts  7.49 us (6%)
    pallas_call x1, Pallas kernels, exchange(): pl.pallas_call(exchange_kernel, out_shape=[big, big, jax.ShapeDtypeStruct...  104 us
    pallas_call x1, Pallas kernels, factor(): pl.pallas_call(factor_kernel, out_shape=[jax.ShapeDtypeStruct((256, 256),...  16 us
    pallas_call x1, Pallas kernels, update(): pl.pallas_call(update_kernel, grid=(8,), out_shape=jax.ShapeDtypeStruct((...  6.69 us
    unnamed x8, local copies, waits for them, and re-layouts  6.04 us

profile of v1, /device:TPU:33, one launch (start us, length us, event | category | flops | bytes accessed | tf_op | source)
XLA Modules:
  0.0 134.8 jit_solution(1187018082855479262)
XLA Ops:
  0.0 0.0 copy-start
  0.0 0.1 pad_add_fusion.1.ids
  0.1 0.6 copy-done
  0.7 0.1 stack_reshape.6
  0.8 0.7 dynamic-slice_bitcast_fusion
  1.5 0.1 stack_reshape.7
  1.6 0.2 select_reduce_fusion
  1.8 0.6 add.48.inv
  2.4 104.3 %exchange.1 = (f32[32,256,128]{2,1,0:T(8,128)}, f32[32,256,128]{2,1,0:T(8,128)}, f32[4,256,128]{2,1,0:T(8,128)}) custom-call(s32[64]{0:T(128)} %add.48.inv, f32[32,256,128]{2,1,0:T(8,128)} %bitcast.18, f32[8,256,128]{2,1,0:T(8,128)} %bitcast.19, f32[8,256,128]{2,1,0:T(8,128)} %bitcast.20), custom_call_target="tpu_custom_call" | custom-call | tf_op jit(solution)/shard_map/exchange/pallas_call | solution.py:326
  106.7 0.0 copy-start.3
  106.7 1.0 copy-done.3
  107.7 16.0 %factor.1 = (f32[256,256]{1,0:T(8,128)S(1)}, f32[128,256]{1,0:T(8,128)S(1)}) custom-call(s32[2]{0:T(128)S(1)} %pad_add_fusion.1.ids, f32[4,256,128]{2,1,0:T(8,128)S(1)} %copy-done.3), custom_call_target="tpu_custom_call" | custom-call | tf_op jit(solution)/shard_map/factor/pallas_call | solution.py:433
  123.8 0.0 copy-start.1
  123.8 2.2 %copy-done.1 = f32[32,256,128]{2,1,0:T(8,128)S(1)} copy-done((f32[32,256,128]{2,1,0:T(8,128)S(1)}, f32[32,256,128]{2,1,0:T(8,128)}, u32[]{:S(2)}) %copy-start.1) | copy-done | bytes 4194328
  126.0 0.0 copy-start.2
  126.0 2.2 %copy-done.2 = f32[32,256,128]{2,1,0:T(8,128)S(1)} copy-done((f32[32,256,128]{2,1,0:T(8,128)S(1)}, f32[32,256,128]{2,1,0:T(8,128)}, u32[]{:S(2)}) %copy-start.2) | copy-done | bytes 4194328
  128.1 6.7 %update.1 = f32[8192,128]{1,0:T(8,128)} custom-call(s32[2]{0:T(128)S(1)} %pad_add_fusion.1.ids, f32[8192,128]{1,0:T(8,128)S(1)} %bitcast.16, f32[8192,128]{1,0:T(8,128)S(1)} %bitcast.17, f32[256,256]{1,0:T(8,128)S(1)} %get-tuple-element.13.weight, f32[128,256]{1,0:T(8,128)S(1)} %get-tuple-element.14.top), custom_call_target="tpu_custom_call" | custom-call | tf_op jit(solution)/shard_map/update/pallas_call | solution.py:461
  (4 shorter events, 0.0 us)
Async XLA Ops:
  0.0 0.7 copy-start
  106.7 1.0 copy-start.3
  123.8 2.2 %copy-start.1 = (f32[32,256,128]{2,1,0:T(8,128)S(1)}, f32[32,256,128]{2,1,0:T(8,128)}, u32[]{:S(2)}) copy-start(f32[32,256,128]{2,1,0:T(8,128)} %get-tuple-element.10) | copy-start | bytes 12582916
  126.0 2.2 %copy-start.2 = (f32[32,256,128]{2,1,0:T(8,128)S(1)}, f32[32,256,128]{2,1,0:T(8,128)}, u32[]{:S(2)}) copy-start(f32[32,256,128]{2,1,0:T(8,128)} %get-tuple-element.11) | copy-start | bytes 12582916

commit v2 on v1

--- a/solution.py
+++ b/solution.py
@@ -15,8 +15,18 @@
 STARTS = tuple(sum(CHUNKS[:i]) for i in range(len(CHUNKS)))
 NCH = len(CHUNKS)
 WINDOW = 3
-PARTS = 32
-SKEW = 2
+TILE = 1024
+GROUPS = 4
+PARTS = 16 * GROUPS
+SKEW = 5
+EXTRA = 14 * GROUPS
+SLOTS = PARTS + 1
+HALF_AT = PARTS // 2 + 6 * SKEW
+LEAD_AT = 3
+PANELS = {3: (0, 5), 4: (5, 10), 5: (10, 16)}
+LEVELS = {6: (0, 4), 7: (4, 8)}
+LATE = 2 * GROUPS
+BEHIND = 1
 
 
 def place():
@@ -45,9 +55,17 @@
     panel_out,
     slab_out,
     window_out,
+    inverse_out,
+    upper_out,
     slab,
     panel,
     win,
+    early,
+    mix,
+    halves,
+    work,
+    upper,
+    inverse,
     load_sem,
     own_sem,
     xs,
@@ -58,6 +76,13 @@
     zr,
     ws,
     wr,
+    es,
+    bs,
+    br,
+    us,
+    ur,
+    vs,
+    vr,
     out_sem,
     *pools,
 ):
@@ -171,9 +196,9 @@
         lax.fori_loop(0, 32, one, 0, unroll=4)
 
     def part(ref, way, t):
-        j8 = t // 2
-        g = t % 2
-        return ref.at[pl.ds(16 * way + 8 * g, 8), pl.ds(pl.multiple_of(16 * j8, 16), 16)]
+        span = 16 // GROUPS
+        base = 16 * way + span * (t % GROUPS)
+        return ref.at[pl.ds(base, span), pl.ds(pl.multiple_of(16 * (t // GROUPS), 16), 16)]
 
     def hop(ref, way, t):
         return remote(
@@ -184,6 +209,60 @@
             prv if way else nxt,
         )
 
+    def early_copy(i):
+        return pltpu.make_async_copy((keep_hbm, give_hbm)[i], early.at[i, pl.ds(0, 8)], es.at[i])
+
+    def swap(i):
+        return remote(mix.at[2 * i + 1 - core], mix.at[4 + i], bs.at[i], br.at[i], mate)
+
+    def across(i):
+        return remote(
+            mix.at[6 + min(i, 1)], mix.at[8 + i], bs.at[2 + i], br.at[2 + i], (far, up, down)[i]
+        )
+
+    def trade():
+        return remote(halves.at[core], halves.at[core], bs.at[5], br.at[5], mate)
+
+    def trade_in():
+        return remote(halves.at[1 - core], halves.at[1 - core], bs.at[5], br.at[5], mate)
+
+    def lead_begin():
+        for i in (0, 1):
+            early_copy(i).wait()
+        for i in (0, 1):
+            for p in (0, 1):
+                mix[2 * i + p] = early[i, inv[64 + 2 * i + p]]
+        for i in (0, 1):
+            swap(i).start()
+        for i in (0, 1):
+            swap(i).wait_recv()
+        mine = mix[core] + mix[4]
+        mix[6] = jnp.where(row < 2, mine + slab[0], mine)
+        mix[7] = mix[2 + core] + mix[5]
+        for i in range(3):
+            across(i).start()
+
+    def lead_end():
+        for i in range(3):
+            across(i).wait_recv()
+        halves[core] = mix[6] + mix[8] + mix[9] + mix[10]
+        trade().start()
+        trade_in().wait_recv()
+        lead = square(halves, 0, 1)
+        work[...] = 0.5 * (lead + lead.T)
+
+    def extra(way):
+        ref = inverse.at[pl.ds(pl.multiple_of(128 * core + 64 * way, 64), 64)]
+        return remote(ref, ref, us.at[way], ur.at[way], prv if way else nxt)
+
+    def extra_mate(way):
+        ref = inverse.at[pl.ds(pl.multiple_of(128 * core + 64 * way, 64), 64)]
+        return remote(ref, ref, vs.at[way], vr.at[way], mate)
+
+    def extra_from_mate(way):
+        ref = inverse.at[pl.ds(pl.multiple_of(128 * (1 - core) + 64 * way, 64), 64)]
+        return remote(ref, ref, vs.at[way], vr.at[way], mate)
+
     for j in range(NCH):
         pools[j][64] = jnp.zeros(pools[j].shape[1:], F32)
     for j in range(WINDOW):
@@ -192,6 +271,10 @@
 
     @pl.when(z == 0)
     def _():
+        for i in (0, 1):
+            early_copy(i).start()
+            early[i, 8] = jnp.zeros((256, 128), F32)
+        lead_begin()
         for j in range(NCH):
             arrive_x(j)
             if j + WINDOW < NCH:
@@ -203,98 +286,146 @@
                     hop(slab, way, t).start()
                 return carry
 
-            lax.fori_loop(STARTS[j] // 4, (STARTS[j] + CHUNKS[j]) // 4, launch, 0)
+            first = STARTS[j] // 8 * GROUPS
+            end = first + CHUNKS[j] // 8 * GROUPS
+            lax.fori_loop(first, end, launch, 0)
+            if end == EXTRA:
+                levels(inverse, upper, *LEVELS[j])
+                for way in (0, 1):
+                    extra(way).start()
+                continue
+            if j == LEAD_AT:
+                lead_end()
+            if j in PANELS:
+                for p in range(*PANELS[j]):
+                    factor_panel(work, upper, 16 * p)
+            if j in LEVELS:
+                levels(inverse, upper, *LEVELS[j])
+
+    half = z // 2
+    owner = 2 * lax.rem(z, 2)
+
+    def spread(h, k):
+        src = panel.at[half, pl.ds(128 * k, 128)]
+        dst = win.at[h, pl.ds(128 * k, 128)]
+        return [
+            remote(src, dst, ws.at[k, i], wr.at[h, k], dev)
+            for i, dev in enumerate((mate, far, far_mate))
+        ]
+
+    def share(k):
+        for h in (0, 1):
+
+            @pl.when(row == owner + h)
+            def _():
+                for c in spread(h, k):
+                    c.start()
+                win[h, pl.ds(128 * k, 128), :] = panel[half, pl.ds(128 * k, 128), :]
 
     @pl.when(z != 0)
     def _():
-        total = PARTS + SKEW * 6
+        total = SLOTS + SKEW * 6
 
         def step(s, carry):
             for way in (0, 1):
                 lag = (7 - z) if way else (z - 1)
-                t = s - SKEW * lag
-
-                @pl.when((t >= 0) & (t < PARTS))
-                def _():
-                    copy = hop(panel, way, t)
+                e = s - SKEW * lag
+                t = e - (e > EXTRA).astype(jnp.int32)
+
+                def pass_on(copy):
                     copy.wait_recv()
 
                     @pl.when(lag < 6)
                     def _():
                         copy.start()
 
+                @pl.when((e >= 0) & (e < SLOTS) & (e != EXTRA))
+                def _():
+                    pass_on(hop(panel, way, t))
+
+                @pl.when(e == EXTRA)
+                def _():
+                    pass_on(extra(way))
+                    extra_mate(way).start()
+
             return carry
 
         done = 0
+        shared = False
         for j in range(NCH):
-            until = 4 + 4 * j
+            until = (STARTS[j] + CHUNKS[j]) // 8 * GROUPS + LATE
+            if until >= HALF_AT and not shared:
+                lax.fori_loop(done, HALF_AT, step, 0)
+                done = HALF_AT
+                share(0)
+                shared = True
             lax.fori_loop(done, until, step, 0)
             done = until
             arrive_x(j)
             if j + WINDOW < NCH:
                 begin_x(j + WINDOW)
-            if j:
-                assemble(j - 1)
+            if j >= BEHIND:
+                assemble(j - BEHIND)
+        if not shared:
+            lax.fori_loop(done, HALF_AT, step, 0)
+            done = HALF_AT
+            share(0)
         lax.fori_loop(done, total, step, 0)
-        assemble(NCH - 1)
-
-    half = z // 2
-    owner = 2 * lax.rem(z, 2)
-
-    def spread(ref, block, slot):
-        src = ref.at[block]
-        out = []
-        for i, dev in enumerate((mate, far, far_mate)):
-            out.append(remote(src, win.at[slot], ws.at[slot // 2, i], wr.at[slot], dev))
-        return out
-
-    def share(ref):
-        @pl.when(row < 2)
-        def _():
-            win[row] = ref[0]
-            for slot in (0, 1):
-
-                @pl.when(row == slot)
-                def _():
-                    for c in spread(ref, 0, slot):
-                        c.start()
-
+        share(1)
+        for j in range(max(0, NCH - BEHIND), NCH):
+            assemble(j)
+
+    pltpu.make_async_copy(slab, slab_out, out_sem.at[1]).start()
+
+    @pl.when(z == 0)
+    def _():
+        pltpu.make_async_copy(slab, panel_out, out_sem.at[0]).start()
+        copy = pltpu.make_async_copy(upper, upper_out, out_sem.at[4])
+        copy.start()
+        win[...] = jnp.zeros_like(win)
+        copy.wait()
+
+    @pl.when(z != 0)
+    def _():
+        pltpu.make_async_copy(panel, panel_out, out_sem.at[0]).start()
+        for way in (0, 1):
+            extra_from_mate(way).wait_recv()
+        for h in (0, 1):
+
+            @pl.when(row != owner + h)
+            def _():
+                for k in (0, 1):
+                    ref = win.at[h, pl.ds(128 * k, 128)]
+                    remote(ref, ref, ws.at[k, 0], wr.at[h, k], mate).wait_recv()
+
+    pltpu.make_async_copy(win, window_out, out_sem.at[2]).start()
+    pltpu.make_async_copy(inverse, inverse_out, out_sem.at[3]).start()
+
+    @pl.when(z == 0)
+    def _():
+        for i in (0, 1):
+            swap(i).wait_send()
+        for i in range(3):
+            across(i).wait_send()
+        trade().wait_send()
+
+    @pl.when(z != 0)
+    def _():
+        for way in (0, 1):
+            extra_mate(way).wait_send()
         for h in (0, 1):
 
             @pl.when(row == owner + h)
             def _():
-                win[2 + h] = ref[half]
-                for c in spread(ref, half, 2 + h):
-                    c.start()
-
-    @pl.when(z == 0)
-    def _():
-        share(slab)
-        pltpu.make_async_copy(slab, panel_out, out_sem.at[0]).start()
-
-    @pl.when(z != 0)
-    def _():
-        share(panel)
-        pltpu.make_async_copy(panel, panel_out, out_sem.at[0]).start()
-
-    pltpu.make_async_copy(slab, slab_out, out_sem.at[1]).start()
-
-    for slot in range(4):
-        holder = slot if slot < 2 else owner + slot - 2
-
-        @pl.when(row != holder)
+                for k in (0, 1):
+                    for c in spread(h, k):
+                        c.wait_send()
+
+    for way in (0, 1):
+
+        @pl.when(z != (1 if way else 7))
         def _():
-            remote(win.at[slot], win.at[slot], ws.at[0, 0], wr.at[slot], mate).wait_recv()
-
-    pltpu.make_async_copy(win, window_out, out_sem.at[2]).start()
-
-    for slot in range(4):
-        holder = slot if slot < 2 else owner + slot - 2
-
-        @pl.when(row == holder)
-        def _():
-            for c in spread(panel, 0, slot):
-                c.wait_send()
+            extra(way).wait_send()
 
     for j in range(NCH):
         for c in send_x(j):
@@ -317,21 +448,29 @@
     pltpu.make_async_copy(panel, panel_out, out_sem.at[0]).wait()
     pltpu.make_async_copy(slab, slab_out, out_sem.at[1]).wait()
     pltpu.make_async_copy(win, window_out, out_sem.at[2]).wait()
+    pltpu.make_async_copy(inverse, inverse_out, out_sem.at[3]).wait()
 
 
 def exchange(inv, front, keep, give):
     big = jax.ShapeDtypeStruct(front.shape, F32)
+    square_shape = jax.ShapeDtypeStruct((256, 256), F32)
     anywhere = pl.BlockSpec(memory_space=pl.ANY)
     dma = pltpu.SemaphoreType.DMA
     return pl.pallas_call(
         exchange_kernel,
-        out_shape=[big, big, jax.ShapeDtypeStruct((4, 256, 128), F32)],
+        out_shape=[big, big, jax.ShapeDtypeStruct((2, 256, 128), F32), square_shape, square_shape],
         in_specs=[pl.BlockSpec(memory_space=pltpu.SMEM)] + [anywhere] * 3,
-        out_specs=[anywhere] * 3,
+        out_specs=[anywhere] * 5,
         scratch_shapes=[
             pltpu.VMEM(front.shape, F32),
             pltpu.VMEM(front.shape, F32),
-            pltpu.VMEM((4, 256, 128), F32),
+            pltpu.VMEM((2, 256, 128), F32),
+            pltpu.VMEM((2, 9, 256, 128), F32),
+            pltpu.VMEM((11, 256, 128), F32),
+            pltpu.VMEM((2, 256, 128), F32),
+            pltpu.VMEM((256, 256), F32),
+            pltpu.VMEM((256, 256), F32),
+            pltpu.VMEM((256, 256), F32),
             dma,
             dma((NCH,)),
             dma((3, NCH)),
@@ -341,12 +480,19 @@
             dma((2, PARTS)),
             dma((2, PARTS)),
             dma((2, 3)),
-            dma((4,)),
-            dma((3,)),
+            dma((2, 2)),
+            dma((2,)),
+            dma((6,)),
+            dma((6,)),
+            dma((2,)),
+            dma((2,)),
+            dma((2,)),
+            dma((2,)),
+            dma((5,)),
         ]
         + [pltpu.VMEM((65, 2 * n, 128), F32) for n in CHUNKS],
         compiler_params=pltpu.CompilerParams(
-            collective_id=0, has_side_effects=True, vmem_limit_bytes=56 << 20
+            collective_id=0, has_side_effects=True, vmem_limit_bytes=40 << 20
         ),
         name="exchange",
     )(inv, front, keep, give)
@@ -384,17 +530,20 @@
         work[j0 + n :, :] = work[j0 + n :, :] - t[j0 + n :, :]
 
 
-def invert_upper(u):
+def levels(inverse, upper, first, end):
     i = lax.broadcasted_iota(jnp.int32, (256, 256), 0)
     j = lax.broadcasted_iota(jnp.int32, (256, 256), 1)
-    inv = jnp.where(i == j, 1.0 / jnp.where(i == j, u, 1.0), 0.0)
-    s = 1
-    while s < 256:
+    u = upper[...]
+    if first == 0:
+        inv = jnp.where(i == j, 1.0 / jnp.where(i == j, u, 1.0), 0.0)
+    else:
+        inv = inverse[...]
+    for level in range(first, end):
+        s = 1 << level
         off = jnp.where((i // (2 * s) == j // (2 * s)) & (i // s < j // s), u, 0.0)
         step = jnp.dot(inv, off, precision=precise, preferred_element_type=F32)
         inv = inv - jnp.dot(step, inv, precision=precise, preferred_element_type=F32)
-        s *= 2
-    return inv
+    inverse[...] = inv
 
 
 def square(ref, a, b):
@@ -404,45 +553,31 @@
     return jnp.concatenate([top, low], axis=0)
 
 
-def factor_kernel(ids, win, weight, top, work, upper):
-    lead = square(win, 0, 1)
-    work[...] = 0.5 * (lead + lead.T)
-    for p in range(16):
-        factor_panel(work, upper, 16 * p)
-    u = upper[...]
-    inv = invert_upper(u)
-
-    @pl.when(ids[0] == 0)
-    def _():
-        weight[...] = -inv
-        low = u.T
-        top[...] = jnp.where(ids[1] == 0, low[:128], low[128:])
-
-    @pl.when(ids[0] != 0)
-    def _():
-        mine = square(win, 2, 3)
-        y = lax.dot_general(
-            inv, mine, (((0,), (1,)), ((), ())), precision=precise, preferred_element_type=F32
-        )
-        weight[...] = jnp.dot(inv, y, precision=precise, preferred_element_type=F32)
-        top[...] = jnp.zeros_like(top)
-
-
-def factor(ids, win):
-    vmem = pl.BlockSpec(memory_space=pltpu.VMEM)
-    return pl.pallas_call(
-        factor_kernel,
-        out_shape=[jax.ShapeDtypeStruct((256, 256), F32), jax.ShapeDtypeStruct((128, 256), F32)],
-        in_specs=[pl.BlockSpec(memory_space=pltpu.SMEM), vmem],
-        out_specs=[vmem, vmem],
-        scratch_shapes=[pltpu.VMEM((256, 256), F32)] * 2,
-        compiler_params=pltpu.CompilerParams(vmem_limit_bytes=40 << 20),
-        name="factor",
-    )(ids, win)
-
-
-def update_kernel(ids, panel, slab, weight, top, out):
-    even, odd = pl.ds(0, 512, 2), pl.ds(1, 512, 2)
+def update_kernel(ids, panel, slab, win, inverse, upper, out, weight, top):
+    even, odd = pl.ds(0, TILE, 2), pl.ds(1, TILE, 2)
+
+    @pl.when(pl.program_id(0) == 0)
+    def _():
+        inv = inverse[...]
+
+        @pl.when(ids[0] == 0)
+        def _():
+            weight[...] = -inv
+            low = upper[...].T
+            top[...] = jnp.where(ids[1] == 0, low[:128], low[128:])
+
+        @pl.when(ids[0] != 0)
+        def _():
+            y = lax.dot_general(
+                inv,
+                square(win, 0, 1),
+                (((0,), (1,)), ((), ())),
+                precision=precise,
+                preferred_element_type=F32,
+            )
+            weight[...] = jnp.dot(inv, y, precision=precise, preferred_element_type=F32)
+            top[...] = jnp.zeros_like(top)
+
     keep = (ids[0] != 0).astype(F32)
     a = jnp.concatenate([panel[even, :], panel[odd, :]], axis=1)
     d = jnp.dot(a, weight[...], precision=precise, preferred_element_type=F32)
@@ -455,24 +590,26 @@
         out[pl.ds(1, 128, 2), :] = top[:, 128:]
 
 
-def update(ids, panel, slab, weight, top):
-    tile = pl.BlockSpec((1024, 128), lambda i: (i, 0))
+def update(ids, panel, slab, win, inverse, upper):
+    tile = pl.BlockSpec((2 * TILE, 128), lambda i: (i, 0))
     whole = pl.BlockSpec((256, 256), lambda i: (0, 0))
     return pl.pallas_call(
         update_kernel,
-        grid=(8,),
+        grid=(4096 // TILE,),
         out_shape=jax.ShapeDtypeStruct((8192, 128), F32),
         in_specs=[
             pl.BlockSpec(memory_space=pltpu.SMEM),
             tile,
             tile,
+            pl.BlockSpec((2, 256, 128), lambda i: (0, 0, 0)),
             whole,
-            pl.BlockSpec((128, 256), lambda i: (0, 0)),
+            whole,
         ],
         out_specs=tile,
+        scratch_shapes=[pltpu.VMEM((256, 256), F32), pltpu.VMEM((128, 256), F32)],
         compiler_params=pltpu.CompilerParams(vmem_limit_bytes=40 << 20),
         name="update",
-    )(ids, panel, slab, weight, top)
+    )(ids, panel, slab, win, inverse, upper)
 
 
 def local(front_slab, child_keep, child_give, map_keep, map_give):
@@ -490,9 +627,14 @@
     hit = tables[:, None, :] == parent[None, :, None]
     inv = (64 + jnp.sum(jnp.where(hit, slot - 64, 0), axis=2)).reshape(64).astype(jnp.int32)
     ids = jnp.stack([col_id, row_id]).astype(jnp.int32)
-    panel, slab, win = exchange(inv, front, keep, give)
-    weight, top = factor(ids, win)
-    out = update(ids, panel.reshape(8192, 128), slab.reshape(8192, 128), weight, top)
+    given = lax.dynamic_index_in_dim(map_give, front_id, 0, keepdims=False)
+    mine = lax.dynamic_index_in_dim(jnp.stack([kept, given]), row_id, 2, keepdims=False)
+    own = jnp.arange(8, dtype=jnp.int32)
+    lead = mine[:, None, :] == jnp.arange(2, dtype=jnp.int32)[None, :, None]
+    lead = (8 + jnp.sum(jnp.where(lead, own - 8, 0), axis=2)).reshape(4).astype(jnp.int32)
+    inv = jnp.concatenate([inv, lead])
+    panel, slab, win, inverse, upper = exchange(inv, front, keep, give)
+    out = update(ids, panel.reshape(8192, 128), slab.reshape(8192, 128), win, inverse, upper)
     return out.reshape(front_slab.shape)
 
 

time: 135 us -> 113 us (0.84)
  Pallas kernels: 127 us -> 109 us
  local copies, waits for them, and re-layouts: 7.49 us -> 3.51 us
    pallas_call x2 -> x1, Pallas kernels: 22.7 us -> 6.82 us  [update(): pl.pallas_call(update_kernel, grid=(4096 // TILE,), out_shape=jax.ShapeDt...]
    unnamed x8 -> x4, local copies, waits for them, and re-layouts: 6.04 us -> 2.46 us
    pallas_call x1, Pallas kernels: 104 us -> 102 us  [exchange(): pl.pallas_call(exchange_kernel, out_shape=[big, big, jax.ShapeDtypeStruct...]
where the time goes in v2:
time: 113 us
  Pallas kernels  109 us (96%)
  local copies, waits for them, and re-layouts  3.51 us (3%)
    pallas_call x1, Pallas kernels, exchange(): pl.pallas_call(exchange_kernel, out_shape=[big, big, jax.ShapeDtypeStruct...  102 us
    pallas_call x1, Pallas kernels, update(): pl.pallas_call(update_kernel, grid=(4096 // TILE,), out_shape=jax.ShapeDt...  6.82 us
    unnamed x4, local copies, waits for them, and re-layouts  2.46 us

profile of v2, /device:TPU:33, one launch (start us, length us, event | category | flops | bytes accessed | tf_op | source)
XLA Modules:
  0.0 112.6 jit_solution(12876265107060291724)
XLA Ops:
  0.0 0.1 pad_add_fusion.1.ids
  0.1 0.7 dynamic-slice_bitcast_fusion
  0.8 0.1 stack_reshape.7
  0.9 0.1 fusion
  1.1 0.1 add.64
  1.1 0.1 stack_reshape.6
  1.2 0.2 select_reduce_fusion
  1.4 0.1 add.61
  1.5 0.1 pad_add_fusion.2.inv
  1.6 0.0 copy-start
  1.6 1.2 %copy-done = f32[1,8,1,128,1,1,256]{6,5,4,3,2,1,0:T(1,128)S(1)} copy-done((f32[1,8,1,128,1,1,256]{6,5,4,3,2,1,0:T(1,128)S(1)}, f32[1,8,1,128,1,1,256]{6,5,4,3,2,1,0:T(1,128)}, u32[]{:S(2)}) %copy-start) | copy-done | bytes 1048600
  2.8 0.0 copy-start.1
  2.8 1.2 %copy-done.1 = f32[1,8,1,128,1,1,256]{6,5,4,3,2,1,0:T(1,128)S(1)} copy-done((f32[1,8,1,128,1,1,256]{6,5,4,3,2,1,0:T(1,128)S(1)}, f32[1,8,1,128,1,1,256]{6,5,4,3,2,1,0:T(1,128)}, u32[]{:S(2)}) %copy-start.1) | copy-done | bytes 1048600
  4.1 101.7 %exchange.1 = (f32[32,256,128]{2,1,0:T(8,128)S(1)}, f32[32,256,128]{2,1,0:T(8,128)S(1)}, f32[2,256,128]{2,1,0:T(8,128)S(1)}, f32[256,256]{1,0:T(8,128)S(1)}, f32[256,256]{1,0:T(8,128)S(1)}) custom-call(s32[68]{0:T(128)S(1)} %pad_add_fusion.2.inv, f32[32,256,128]{2,1,0:T(8,128)} %bitcast.20, f32[8,256,128]{2,1,0:T(8,128)S(1)} %bitcast.18, ...), custom_call_target="tpu_custom_call" | custom-call | tf_op jit(solution)/shard_map/exchange/pallas_call | solution.py:459
  105.8 6.8 %update.1 = f32[8192,128]{1,0:T(8,128)} custom-call(s32[2]{0:T(128)S(1)} %pad_add_fusion.1.ids, f32[8192,128]{1,0:T(8,128)S(1)} %bitcast.16, f32[8192,128]{1,0:T(8,128)S(1)} %bitcast.17, f32[2,256,128]{2,1,0:T(8,128)S(1)} %get-tuple-element.12.win, f32[256,256]{1,0:T(8,128)S(1)} %get-tuple-element.13.inverse, f32[256,256]{1,0:T(8,128)S(1)} %get-tuple-element.14.upper), custom_call_target="tpu_custom_call" | custom-call | tf_op jit(solution)/shard_map/update/pallas_call | solution.py:596
  (7 shorter events, 0.0 us)
Async XLA Ops:
  1.6 1.2 %copy-start = (f32[1,8,1,128,1,1,256]{6,5,4,3,2,1,0:T(1,128)S(1)}, f32[1,8,1,128,1,1,256]{6,5,4,3,2,1,0:T(1,128)}, u32[]{:S(2)}) copy-start(f32[1,8,1,128,1,1,256]{6,5,4,3,2,1,0:T(1,128)} %param.6) | copy-start | bytes 3145732
  2.8 1.2 %copy-start.1 = (f32[1,8,1,128,1,1,256]{6,5,4,3,2,1,0:T(1,128)S(1)}, f32[1,8,1,128,1,1,256]{6,5,4,3,2,1,0:T(1,128)}, u32[]{:S(2)}) copy-start(f32[1,8,1,128,1,1,256]{6,5,4,3,2,1,0:T(1,128)} %param.7) | copy-start | bytes 3145732

commit v3 on v2

--- a/solution.py
+++ b/solution.py
@@ -11,7 +11,7 @@
 BF16 = jnp.bfloat16
 precise = lax.Precision.HIGHEST
 
-CHUNKS = (8, 8, 16, 16, 16, 16, 16, 16, 16)
+CHUNKS = (8, 8, 16, 16, 16, 16, 16, 16, 8, 8)
 STARTS = tuple(sum(CHUNKS[:i]) for i in range(len(CHUNKS)))
 NCH = len(CHUNKS)
 WINDOW = 3
@@ -19,9 +19,11 @@
 GROUPS = 4
 PARTS = 16 * GROUPS
 SKEW = 5
-EXTRA = 14 * GROUPS
-SLOTS = PARTS + 1
-HALF_AT = PARTS // 2 + 6 * SKEW
+ROUND = 14 * GROUPS
+BOTH = 2 * (PARTS - ROUND)
+SLOTS = ROUND + 2 + BOTH
+CUT = 96
+CUT_AT = CUT // 8 * GROUPS + 6 * SKEW
 LEAD_AT = 3
 PANELS = {3: (0, 5), 4: (5, 10), 5: (10, 16)}
 LEVELS = {6: (0, 4), 7: (4, 8)}
@@ -83,7 +85,10 @@
     ur,
     vs,
     vr,
+    ds,
+    dr,
     out_sem,
+    row_sem,
     *pools,
 ):
     x, y, z, core = place()
@@ -251,17 +256,35 @@
         lead = square(halves, 0, 1)
         work[...] = 0.5 * (lead + lead.T)
 
-    def extra(way):
-        ref = inverse.at[pl.ds(pl.multiple_of(128 * core + 64 * way, 64), 64)]
-        return remote(ref, ref, us.at[way], ur.at[way], prv if way else nxt)
-
-    def extra_mate(way):
-        ref = inverse.at[pl.ds(pl.multiple_of(128 * core + 64 * way, 64), 64)]
-        return remote(ref, ref, vs.at[way], vr.at[way], mate)
-
-    def extra_from_mate(way):
-        ref = inverse.at[pl.ds(pl.multiple_of(128 * (1 - core) + 64 * way, 64), 64)]
-        return remote(ref, ref, vs.at[way], vr.at[way], mate)
+    def quarter(c, q):
+        return inverse.at[pl.ds(pl.multiple_of(128 * c + 64 * q, 64), 64)]
+
+    def extra(way, q):
+        ref = quarter(core, q)
+        return remote(ref, ref, us.at[way, q], ur.at[q], prv if way else nxt)
+
+    def extra_mate(q):
+        ref = quarter(core, q)
+        return remote(ref, ref, vs.at[q], vr.at[q], mate)
+
+    def extra_from_mate(q):
+        ref = quarter(1 - core, q)
+        return remote(ref, ref, vs.at[q], vr.at[q], mate)
+
+    def both_part(ref, d):
+        span = 16 // GROUPS
+        row8 = ROUND // GROUPS + d // (2 * GROUPS)
+        return ref.at[
+            pl.ds(span * (d % (2 * GROUPS)), span), pl.ds(pl.multiple_of(16 * row8, 16), 16)
+        ]
+
+    def both(ref, way, d):
+        return remote(
+            both_part(ref, d), both_part(panel, d), ds.at[way, d], dr.at[d], prv if way else nxt
+        )
+
+    def row_copy(j, dst):
+        return pltpu.make_async_copy(slab.at[:, rows(j)], dst.at[:, rows(j)], row_sem.at[j])
 
     for j in range(NCH):
         pools[j][64] = jnp.zeros(pools[j].shape[1:], F32)
@@ -280,19 +303,29 @@
             if j + WINDOW < NCH:
                 begin_x(j + WINDOW)
             assemble(j)
+            row_copy(j, panel_out).start()
 
             def launch(t, carry):
                 for way in (0, 1):
                     hop(slab, way, t).start()
                 return carry
 
+            def launch_both(d, carry):
+                for way in (0, 1):
+                    both(slab, way, d).start()
+                return carry
+
             first = STARTS[j] // 8 * GROUPS
             end = first + CHUNKS[j] // 8 * GROUPS
-            lax.fori_loop(first, end, launch, 0)
-            if end == EXTRA:
+            if end <= ROUND:
+                lax.fori_loop(first, end, launch, 0)
+            else:
+                lax.fori_loop(2 * (first - ROUND), 2 * (end - ROUND), launch_both, 0)
+            if end == ROUND:
                 levels(inverse, upper, *LEVELS[j])
                 for way in (0, 1):
-                    extra(way).start()
+                    for q in (0, 1):
+                        extra(way, q).start()
                 continue
             if j == LEAD_AT:
                 lead_end()
@@ -305,14 +338,22 @@
     half = z // 2
     owner = 2 * lax.rem(z, 2)
 
+    def cut(k):
+        return pl.ds(0, 2 * CUT) if k == 0 else pl.ds(2 * CUT, 256 - 2 * CUT)
+
     def spread(h, k):
-        src = panel.at[half, pl.ds(128 * k, 128)]
-        dst = win.at[h, pl.ds(128 * k, 128)]
+        src = panel.at[half, cut(k)]
+        dst = win.at[h, cut(k)]
         return [
             remote(src, dst, ws.at[k, i], wr.at[h, k], dev)
             for i, dev in enumerate((mate, far, far_mate))
         ]
 
+    def panel_copy(k):
+        return pltpu.make_async_copy(
+            panel.at[:, cut(k)], panel_out.at[:, cut(k)], out_sem.at[k]
+        )
+
     def share(k):
         for h in (0, 1):
 
@@ -320,33 +361,53 @@
             def _():
                 for c in spread(h, k):
                     c.start()
-                win[h, pl.ds(128 * k, 128), :] = panel[half, pl.ds(128 * k, 128), :]
+                win[h, cut(k), :] = panel[half, cut(k), :]
+
+        panel_copy(k).start()
 
     @pl.when(z != 0)
     def _():
-        total = SLOTS + SKEW * 6
+        total = max(SLOTS + SKEW * 3, ROUND + SKEW * 6)
 
         def step(s, carry):
             for way in (0, 1):
                 lag = (7 - z) if way else (z - 1)
-                e = s - SKEW * lag
-                t = e - (e > EXTRA).astype(jnp.int32)
-
-                def pass_on(copy):
+                near = (z > 4) if way else (z <= 4)
+                end = 5 if way else 4
+                t = s - SKEW * lag
+
+                @pl.when((t >= 0) & (t < ROUND))
+                def _():
+                    copy = hop(panel, way, t)
                     copy.wait_recv()
 
                     @pl.when(lag < 6)
                     def _():
                         copy.start()
 
-                @pl.when((e >= 0) & (e < SLOTS) & (e != EXTRA))
+                @pl.when(near & (t >= ROUND) & (t < SLOTS))
                 def _():
-                    pass_on(hop(panel, way, t))
-
-                @pl.when(e == EXTRA)
-                def _():
-                    pass_on(extra(way))
-                    extra_mate(way).start()
+                    for q in (0, 1):
+
+                        @pl.when(t == ROUND + q)
+                        def _():
+                            copy = extra(way, q)
+                            copy.wait_recv()
+
+                            @pl.when(z != end)
+                            def _():
+                                copy.start()
+
+                            extra_mate(q).start()
+
+                    @pl.when(t >= ROUND + 2)
+                    def _():
+                        copy = both(panel, way, t - ROUND - 2)
+                        copy.wait_recv()
+
+                        @pl.when(z != end)
+                        def _():
+                            copy.start()
 
             return carry
 
@@ -354,9 +415,9 @@
         shared = False
         for j in range(NCH):
             until = (STARTS[j] + CHUNKS[j]) // 8 * GROUPS + LATE
-            if until >= HALF_AT and not shared:
-                lax.fori_loop(done, HALF_AT, step, 0)
-                done = HALF_AT
+            if until >= CUT_AT and not shared:
+                lax.fori_loop(done, CUT_AT, step, 0)
+                done = CUT_AT
                 share(0)
                 shared = True
             lax.fori_loop(done, until, step, 0)
@@ -366,20 +427,19 @@
                 begin_x(j + WINDOW)
             if j >= BEHIND:
                 assemble(j - BEHIND)
+                row_copy(j - BEHIND, slab_out).start()
         if not shared:
-            lax.fori_loop(done, HALF_AT, step, 0)
-            done = HALF_AT
+            lax.fori_loop(done, CUT_AT, step, 0)
+            done = CUT_AT
             share(0)
         lax.fori_loop(done, total, step, 0)
         share(1)
         for j in range(max(0, NCH - BEHIND), NCH):
             assemble(j)
-
-    pltpu.make_async_copy(slab, slab_out, out_sem.at[1]).start()
+            row_copy(j, slab_out).start()
 
     @pl.when(z == 0)
     def _():
-        pltpu.make_async_copy(slab, panel_out, out_sem.at[0]).start()
         copy = pltpu.make_async_copy(upper, upper_out, out_sem.at[4])
         copy.start()
         win[...] = jnp.zeros_like(win)
@@ -387,15 +447,14 @@
 
     @pl.when(z != 0)
     def _():
-        pltpu.make_async_copy(panel, panel_out, out_sem.at[0]).start()
-        for way in (0, 1):
-            extra_from_mate(way).wait_recv()
+        for q in (0, 1):
+            extra_from_mate(q).wait_recv()
         for h in (0, 1):
 
             @pl.when(row != owner + h)
             def _():
                 for k in (0, 1):
-                    ref = win.at[h, pl.ds(128 * k, 128)]
+                    ref = win.at[h, cut(k)]
                     remote(ref, ref, ws.at[k, 0], wr.at[h, k], mate).wait_recv()
 
     pltpu.make_async_copy(win, window_out, out_sem.at[2]).start()
@@ -411,8 +470,10 @@
 
     @pl.when(z != 0)
     def _():
-        for way in (0, 1):
-            extra_mate(way).wait_send()
+        for q in (0, 1):
+            extra_mate(q).wait_send()
+        for k in (0, 1):
+            panel_copy(k).wait()
         for h in (0, 1):
 
             @pl.when(row == owner + h)
@@ -423,9 +484,16 @@
 
     for way in (0, 1):
 
-        @pl.when(z != (1 if way else 7))
+        @pl.when(((z == 0) | (z > 5)) if way else (z < 4))
         def _():
-            extra(way).wait_send()
+            for q in (0, 1):
+                extra(way, q).wait_send()
+
+            def drain_both(d, carry):
+                both(panel, way, d).wait_send()
+                return carry
+
+            lax.fori_loop(0, BOTH, drain_both, 0)
 
     for j in range(NCH):
         for c in send_x(j):
@@ -444,9 +512,9 @@
 
         return carry
 
-    lax.fori_loop(0, PARTS, drain, 0)
-    pltpu.make_async_copy(panel, panel_out, out_sem.at[0]).wait()
-    pltpu.make_async_copy(slab, slab_out, out_sem.at[1]).wait()
+    lax.fori_loop(0, ROUND, drain, 0)
+    for j in range(NCH):
+        row_copy(j, slab_out).wait()
     pltpu.make_async_copy(win, window_out, out_sem.at[2]).wait()
     pltpu.make_async_copy(inverse, inverse_out, out_sem.at[3]).wait()
 
@@ -459,7 +527,7 @@
     return pl.pallas_call(
         exchange_kernel,
         out_shape=[big, big, jax.ShapeDtypeStruct((2, 256, 128), F32), square_shape, square_shape],
-        in_specs=[pl.BlockSpec(memory_space=pltpu.SMEM)] + [anywhere] * 3,
+        in_specs=[pl.BlockSpec(memory_space=pltpu.SMEM)] + [pl.BlockSpec(memory_space=pltpu.HBM)] * 3,
         out_specs=[anywhere] * 5,
         scratch_shapes=[
             pltpu.VMEM(front.shape, F32),
@@ -477,18 +545,21 @@
             dma((3, NCH)),
             dma((4, NCH)),
             dma((4, NCH)),
-            dma((2, PARTS)),
-            dma((2, PARTS)),
+            dma((2, ROUND)),
+            dma((2, ROUND)),
             dma((2, 3)),
             dma((2, 2)),
             dma((2,)),
             dma((6,)),
             dma((6,)),
+            dma((2, 2)),
             dma((2,)),
             dma((2,)),
             dma((2,)),
-            dma((2,)),
+            dma((2, BOTH)),
+            dma((BOTH,)),
             dma((5,)),
+            dma((NCH,)),
         ]
         + [pltpu.VMEM((65, 2 * n, 128), F32) for n in CHUNKS],
         compiler_params=pltpu.CompilerParams(
@@ -578,11 +649,10 @@
             weight[...] = jnp.dot(inv, y, precision=precise, preferred_element_type=F32)
             top[...] = jnp.zeros_like(top)
 
-    keep = (ids[0] != 0).astype(F32)
     a = jnp.concatenate([panel[even, :], panel[odd, :]], axis=1)
     d = jnp.dot(a, weight[...], precision=precise, preferred_element_type=F32)
-    out[even, :] = keep * slab[even, :] - d[:, :128]
-    out[odd, :] = keep * slab[odd, :] - d[:, 128:]
+    out[even, :] = jnp.where(ids[0] != 0, slab[even, :], 0.0) - d[:, :128]
+    out[odd, :] = jnp.where(ids[0] != 0, slab[odd, :], 0.0) - d[:, 128:]
 
     @pl.when((pl.program_id(0) == 0) & (ids[1] < 2))
     def _():
@@ -616,9 +686,10 @@
     front_id = lax.axis_index("front")
     row_id = lax.axis_index("row")
     col_id = lax.axis_index("col")
-    front = front_slab.reshape(32, 256, 128)
-    keep = child_keep.reshape(8, 256, 128)
-    give = child_give.reshape(8, 256, 128)
+    front, keep, give = (
+        pltpu.with_memory_space_constraint(a.reshape(n, 256, 128), pltpu.HBM)
+        for a, n in ((front_slab, 32), (child_keep, 8), (child_give, 8))
+    )
     kept = lax.dynamic_index_in_dim(map_keep, front_id, 0, keepdims=False)
     moved = lax.dynamic_index_in_dim(map_give, front_id ^ 1, 0, keepdims=False)
     tables = jnp.stack([kept.T.reshape(32), moved.T.reshape(32)])

time: 113 us -> 104 us (0.920)
  Pallas kernels: 109 us -> 103 us
  local copies, waits for them, and re-layouts: 3.51 us -> 1.05 us
    pallas_call x1, Pallas kernels: 102 us -> 95.8 us  [exchange(): pl.pallas_call(exchange_kernel, out_shape=[big, big, jax.ShapeDtypeStruct...]
    unnamed x4 -> x0, local copies, waits for them, and re-layouts: 2.46 us -> none
where the time goes in v3:
time: 104 us
  Pallas kernels  103 us (99%)
  local copies, waits for them, and re-layouts  1.05 us (1%)
    pallas_call x1, Pallas kernels, exchange(): pl.pallas_call(exchange_kernel, out_shape=[big, big, jax.ShapeDtypeStruct...  95.8 us
    pallas_call x1, Pallas kernels, update(): pl.pallas_call(update_kernel, grid=(4096 // TILE,), out_shape=jax.ShapeDt...  6.83 us

profile of v3, /device:TPU:33, one launch (start us, length us, event | category | flops | bytes accessed | tf_op | source)
XLA Modules:
  0.0 104.3 jit_solution(8896372917227745228)
XLA Ops:
  0.0 0.1 pad_add_fusion.1.ids
  0.1 0.7 dynamic-slice_bitcast_fusion
  0.8 0.1 stack_reshape.7
  0.9 0.1 fusion
  1.1 0.1 add.64
  1.1 0.1 stack_reshape.6
  1.2 0.2 select_reduce_fusion
  1.4 0.1 add.61
  1.5 0.1 pad_add_fusion.2.inv
  1.6 95.8 %exchange.1 = (f32[32,256,128]{2,1,0:T(8,128)S(1)}, f32[32,256,128]{2,1,0:T(8,128)S(1)}, f32[2,256,128]{2,1,0:T(8,128)S(1)}, f32[256,256]{1,0:T(8,128)S(1)}, f32[256,256]{1,0:T(8,128)S(1)}) custom-call(s32[68]{0:T(128)S(1)} %pad_add_fusion.2.inv, f32[32,256,128]{2,1,0:T(8,128)} %bitcast.18, f32[8,256,128]{2,1,0:T(8,128)} %bitcast.19, f32[8,256,128]{2,1,0:T(8,128)} %bitcast.20), custom_call_target="tpu_custom_call" | custom-call | tf_op jit(solution)/shard_map/exchange/pallas_call | solution.py:527
  97.4 6.8 %update.1 = f32[8192,128]{1,0:T(8,128)} custom-call(s32[2]{0:T(128)S(1)} %pad_add_fusion.1.ids, f32[8192,128]{1,0:T(8,128)S(1)} %bitcast.16, f32[8192,128]{1,0:T(8,128)S(1)} %bitcast.17, f32[2,256,128]{2,1,0:T(8,128)S(1)} %get-tuple-element.12.win, f32[256,256]{1,0:T(8,128)S(1)} %get-tuple-element.13.inverse, f32[256,256]{1,0:T(8,128)S(1)} %get-tuple-element.14.upper), custom_call_target="tpu_custom_call" | custom-call | tf_op jit(solution)/shard_map/update/pallas_call | solution.py:666
  (7 shorter events, 0.0 us)

commit v4 on v3

--- a/solution.py
+++ b/solution.py
@@ -24,9 +24,10 @@
 SLOTS = ROUND + 2 + BOTH
 CUT = 96
 CUT_AT = CUT // 8 * GROUPS + 6 * SKEW
-LEAD_AT = 3
-PANELS = {3: (0, 5), 4: (5, 10), 5: (10, 16)}
-LEVELS = {6: (0, 4), 7: (4, 8)}
+LEAD_AT = 4
+LEAD_STEP = 12
+PANELS = {4: (0, 5), 5: (5, 10), 6: (10, 16)}
+LEVELS = {7: (0, 8)}
 LATE = 2 * GROUPS
 BEHIND = 1
 
@@ -220,10 +221,38 @@
     def swap(i):
         return remote(mix.at[2 * i + 1 - core], mix.at[4 + i], bs.at[i], br.at[i], mate)
 
-    def across(i):
-        return remote(
-            mix.at[6 + min(i, 1)], mix.at[8 + i], bs.at[2 + i], br.at[2 + i], (far, up, down)[i]
-        )
+    lend_keep = remote(mix.at[6], mix.at[0], bs.at[2], br.at[0], nxt)
+    lend_give = remote(mix.at[7], mix.at[0], bs.at[3], br.at[0], prv)
+    keep_far = remote(mix.at[0], mix.at[1], bs.at[0], br.at[1], far)
+    keep_back = remote(mix.at[1], mix.at[8], bs.at[1], br.at[2], prv)
+    give_up = remote(mix.at[0], mix.at[1], bs.at[0], br.at[1], up)
+    give_down = remote(mix.at[0], mix.at[2], bs.at[1], br.at[2], down)
+    give_back = remote(mix.at[3], mix.at[9], bs.at[2], br.at[3], nxt)
+
+    def lend_across():
+        @pl.when(z == 1)
+        def _():
+            lend_keep.wait_recv()
+            keep_far.start()
+
+        @pl.when(z == 7)
+        def _():
+            lend_give.wait_recv()
+            give_up.start()
+            give_down.start()
+
+    def lend_back():
+        @pl.when(z == 1)
+        def _():
+            keep_far.wait_recv()
+            keep_back.start()
+
+        @pl.when(z == 7)
+        def _():
+            give_up.wait_recv()
+            give_down.wait_recv()
+            mix[3] = mix[1] + mix[2]
+            give_back.start()
 
     def trade():
         return remote(halves.at[core], halves.at[core], bs.at[5], br.at[5], mate)
@@ -244,13 +273,13 @@
         mine = mix[core] + mix[4]
         mix[6] = jnp.where(row < 2, mine + slab[0], mine)
         mix[7] = mix[2 + core] + mix[5]
-        for i in range(3):
-            across(i).start()
+        lend_keep.start()
+        lend_give.start()
 
     def lead_end():
-        for i in range(3):
-            across(i).wait_recv()
-        halves[core] = mix[6] + mix[8] + mix[9] + mix[10]
+        keep_back.wait_recv()
+        give_back.wait_recv()
+        halves[core] = mix[6] + mix[8] + mix[9]
         trade().start()
         trade_in().wait_recv()
         lead = square(halves, 0, 1)
@@ -288,6 +317,7 @@
 
     for j in range(NCH):
         pools[j][64] = jnp.zeros(pools[j].shape[1:], F32)
+    lend_across()
     for j in range(WINDOW):
         begin_x(j)
     load.wait()
@@ -411,7 +441,9 @@
 
             return carry
 
-        done = 0
+        lax.fori_loop(0, LEAD_STEP, step, 0)
+        lend_back()
+        done = LEAD_STEP
         shared = False
         for j in range(NCH):
             until = (STARTS[j] + CHUNKS[j]) // 8 * GROUPS + LATE
@@ -420,8 +452,9 @@
                 done = CUT_AT
                 share(0)
                 shared = True
-            lax.fori_loop(done, until, step, 0)
-            done = until
+            if until > done:
+                lax.fori_loop(done, until, step, 0)
+                done = until
             arrive_x(j)
             if j + WINDOW < NCH:
                 begin_x(j + WINDOW)
@@ -464,9 +497,20 @@
     def _():
         for i in (0, 1):
             swap(i).wait_send()
-        for i in range(3):
-            across(i).wait_send()
+        lend_keep.wait_send()
+        lend_give.wait_send()
         trade().wait_send()
+
+    @pl.when(z == 1)
+    def _():
+        keep_far.wait_send()
+        keep_back.wait_send()
+
+    @pl.when(z == 7)
+    def _():
+        give_up.wait_send()
+        give_down.wait_send()
+        give_back.wait_send()
 
     @pl.when(z != 0)
     def _():
@@ -534,7 +578,7 @@
             pltpu.VMEM(front.shape, F32),
             pltpu.VMEM((2, 256, 128), F32),
             pltpu.VMEM((2, 9, 256, 128), F32),
-            pltpu.VMEM((11, 256, 128), F32),
+            pltpu.VMEM((10, 256, 128), F32),
             pltpu.VMEM((2, 256, 128), F32),
             pltpu.VMEM((256, 256), F32),
             pltpu.VMEM((256, 256), F32),

time: 104 us -> 100 us (0.962)
  Pallas kernels: 103 us -> 98.4 us
    pallas_call x1, Pallas kernels: 95.8 us -> 91.5 us  [exchange(): pl.pallas_call(exchange_kernel, out_shape=[big, big, jax.ShapeDtypeStruct...]
where the time goes in v4:
time: 100 us
  Pallas kernels  98.4 us (98%)
  local copies, waits for them, and re-layouts  1.05 us (1%)
    pallas_call x1, Pallas kernels, exchange(): pl.pallas_call(exchange_kernel, out_shape=[big, big, jax.ShapeDtypeStruct...  91.5 us
    pallas_call x1, Pallas kernels, update(): pl.pallas_call(update_kernel, grid=(4096 // TILE,), out_shape=jax.ShapeDt...  6.83 us

profile of v4, /device:TPU:33, one launch (start us, length us, event | category | flops | bytes accessed | tf_op | source)
XLA Modules:
  0.0 100.0 jit_solution(10580098970812572230)
XLA Ops:
  0.0 0.1 pad_add_fusion.1.ids
  0.1 0.7 dynamic-slice_bitcast_fusion
  0.8 0.1 stack_reshape.7
  0.9 0.1 fusion
  1.1 0.1 add.64
  1.1 0.1 stack_reshape.6
  1.2 0.2 select_reduce_fusion
  1.4 0.1 add.61
  1.5 0.1 pad_add_fusion.2.inv
  1.6 91.5 %exchange.1 = (f32[32,256,128]{2,1,0:T(8,128)S(1)}, f32[32,256,128]{2,1,0:T(8,128)S(1)}, f32[2,256,128]{2,1,0:T(8,128)S(1)}, f32[256,256]{1,0:T(8,128)S(1)}, f32[256,256]{1,0:T(8,128)S(1)}) custom-call(s32[68]{0:T(128)S(1)} %pad_add_fusion.2.inv, f32[32,256,128]{2,1,0:T(8,128)} %bitcast.18, f32[8,256,128]{2,1,0:T(8,128)} %bitcast.19, f32[8,256,128]{2,1,0:T(8,128)} %bitcast.20), custom_call_target="tpu_custom_call" | custom-call | tf_op jit(solution)/shard_map/exchange/pallas_call | solution.py:571
  93.1 6.8 %update.1 = f32[8192,128]{1,0:T(8,128)} custom-call(s32[2]{0:T(128)S(1)} %pad_add_fusion.1.ids, f32[8192,128]{1,0:T(8,128)S(1)} %bitcast.16, f32[8192,128]{1,0:T(8,128)S(1)} %bitcast.17, f32[2,256,128]{2,1,0:T(8,128)S(1)} %get-tuple-element.12.win, f32[256,256]{1,0:T(8,128)S(1)} %get-tuple-element.13.inverse, f32[256,256]{1,0:T(8,128)S(1)} %get-tuple-element.14.upper), custom_call_target="tpu_custom_call" | custom-call | tf_op jit(solution)/shard_map/update/pallas_call | solution.py:710
  (7 shorter events, 0.0 us)

commit v5 on v4

--- a/solution.py
+++ b/solution.py
@@ -482,6 +482,10 @@
     def _():
         for q in (0, 1):
             extra_from_mate(q).wait_recv()
+        u = inverse[...]
+        work[...] = lax.dot_general(
+            u, u, (((1,), (1,)), ((), ())), precision=precise, preferred_element_type=F32
+        )
         for h in (0, 1):
 
             @pl.when(row != owner + h)
@@ -491,7 +495,15 @@
                     remote(ref, ref, ws.at[k, 0], wr.at[h, k], mate).wait_recv()
 
     pltpu.make_async_copy(win, window_out, out_sem.at[2]).start()
-    pltpu.make_async_copy(inverse, inverse_out, out_sem.at[3]).start()
+
+    @pl.when(z == 0)
+    def _():
+        pltpu.make_async_copy(inverse, inverse_out, out_sem.at[3]).start()
+
+    @pl.when(z != 0)
+    def _():
+        pltpu.make_async_copy(work, inverse_out, out_sem.at[3]).start()
+
 
     @pl.when(z == 0)
     def _():
@@ -683,14 +695,13 @@
 
         @pl.when(ids[0] != 0)
         def _():
-            y = lax.dot_general(
+            weight[...] = lax.dot_general(
                 inv,
                 square(win, 0, 1),
-                (((0,), (1,)), ((), ())),
+                (((1,), (1,)), ((), ())),
                 precision=precise,
                 preferred_element_type=F32,
             )
-            weight[...] = jnp.dot(inv, y, precision=precise, preferred_element_type=F32)
             top[...] = jnp.zeros_like(top)
 
     a = jnp.concatenate([panel[even, :], panel[odd, :]], axis=1)

time: 100 us -> 99.4 us (level)
  no operation moved by 1% of the time
where the time goes in v5:
time: 99.4 us; the launch traced here: 99.3 us
  Pallas kernels  97.7 us (98%)
  local copies, waits for them, and re-layouts  1.05 us (1%)
    pallas_call x1, Pallas kernels, exchange(): pl.pallas_call(exchange_kernel, out_shape=[big, big, jax.ShapeDtypeStruct...  91.5 us
    pallas_call x1, Pallas kernels, update(): pl.pallas_call(update_kernel, grid=(4096 // TILE,), out_shape=jax.ShapeDt...  6.13 us

profile of v5, /device:TPU:33, one launch (start us, length us, event | category | flops | bytes accessed | tf_op | source)
XLA Modules:
  0.0 99.3 jit_solution(10602042375758719026)
XLA Ops:
  0.0 0.1 pad_add_fusion.1.ids
  0.1 0.7 dynamic-slice_bitcast_fusion
  0.8 0.1 stack_reshape.7
  0.9 0.1 fusion
  1.1 0.1 add.64
  1.1 0.1 stack_reshape.6
  1.2 0.2 select_reduce_fusion
  1.4 0.1 add.61
  1.5 0.1 pad_add_fusion.2.inv
  1.6 91.5 %exchange.1 = (f32[32,256,128]{2,1,0:T(8,128)S(1)}, f32[32,256,128]{2,1,0:T(8,128)S(1)}, f32[2,256,128]{2,1,0:T(8,128)S(1)}, f32[256,256]{1,0:T(8,128)S(1)}, f32[256,256]{1,0:T(8,128)S(1)}) custom-call(s32[68]{0:T(128)S(1)} %pad_add_fusion.2.inv, f32[32,256,128]{2,1,0:T(8,128)} %bitcast.18, f32[8,256,128]{2,1,0:T(8,128)} %bitcast.19, f32[8,256,128]{2,1,0:T(8,128)} %bitcast.20), custom_call_target="tpu_custom_call" | custom-call | tf_op jit(solution)/shard_map/exchange/pallas_call | solution.py:583
  93.1 6.1 %update.1 = f32[8192,128]{1,0:T(8,128)} custom-call(s32[2]{0:T(128)S(1)} %pad_add_fusion.1.ids, f32[8192,128]{1,0:T(8,128)S(1)} %bitcast.16, f32[8192,128]{1,0:T(8,128)S(1)} %bitcast.17, f32[2,256,128]{2,1,0:T(8,128)S(1)} %get-tuple-element.12.win, f32[256,256]{1,0:T(8,128)S(1)} %get-tuple-element.13.inverse, f32[256,256]{1,0:T(8,128)S(1)} %get-tuple-element.14.upper), custom_call_target="tpu_custom_call" | custom-call | tf_op jit(solution)/shard_map/update/pallas_call | solution.py:721
  (7 shorter events, 0.0 us)
